TPU v7x, 32 devices: a whole 2x2x4 slice. The times are simulated.
32 devices in a mesh: groups: 2 (over y), blk: 4 (over z), tgt: 4 (over x, core).
Axes of the slice: x: 2, y: 2, z: 4, core: 2. Of those that a mesh axis runs over, the one named last changes fastest.
Arguments:
- positions: float32 [3, 9984], P(None, ('groups', 'blk', 'tgt')), parts along dimension 1
- forces: float32 [3, 9984], P(None, ('groups', 'blk', 'tgt')), parts along dimension 1, may hold values from -8 to 8
- owner_map: int32 [32], P('groups'), parts along dimension 0, may hold values from 0 to 15, as said below
- near_target: int32 [4096], P(('groups', 'blk', 'tgt')), parts along dimension 0, may hold values from 0 to 15, as said below
- near_source: int32 [4096], P(('groups', 'blk', 'tgt')), parts along dimension 0, may hold values from 0 to 15, as said below
- near_patch: int32 [4096], P(('groups', 'blk', 'tgt')), parts along dimension 0, may hold values from 0 to 31
- patch_rows: int32 [32, 256], replicated, may hold values from 0 to 2663, as said below
- zone_rows: int32 [32, 128], replicated, may hold values from 0 to 311, as said below
Outputs:
- velocity: float32 [3, 9984], P(None, ('groups', 'blk', 'tgt')), parts along dimension 1
- patch_velocity: float32 [3, 9984], P(None, ('groups', 'blk', 'tgt')), parts along dimension 1
There are 2 independent parts, one for each index of `groups`. A program takes and returns all parts, laid end to end along the dimension named above; an argument that names none is the same for every part. Nothing has to cross between parts.
Inputs may be any that keep to these rules, and one draw needn't show every extreme that they name: owner_map is a permutation; the vesicle in slot s is stored on the device of index s // 1 along blk+tgt. `near_source`: the 128 entries held by one device of blk+tgt name source vesicles stored on that device. `near_target`: among the 128 entries held by one device, at most 16 name target vesicles stored on any one device; one device, drawn anew, is named exactly 16 times by every device's entries. `patch_rows`: row p lists the nodes of a block of 16 x 16 cells of the 37 x 72 upsampled grid, node index = polar row * 72 + azimuthal column, azimuthal columns wrapping. `zone_rows`: row p lists the nodes of a block of 8 x 16 cells of the 13 x 24 coarse grid, node index = polar row * 24 + azimuthal column, azimuthal columns wrapping.
All inputs are finite; a program needn't handle non-finite values.
Results may differ from a plain program's by a relative error of at most 0.0003.
Values sent between devices are 32-bit elements; how exact they have to be, the bound alone decides.
A program may use at most 128 MiB of HBM per device.

v0:
```python
import math

import jax
import jax.numpy as jnp
import numpy as np
from jax import lax
from jax.sharding import PartitionSpec as P

THETA = 13
PHI = 24
FINE_THETA = 37
FINE_PHI = 72
NODES = 312
FINE = 2664


FAR_BLOB = 0.09
NEAR_BLOB = 0.0025
STOKES_FACTOR = 1.0 / (8.0 * math.pi)


def polar_weights(coarse, fine_count):
    weights = np.zeros((fine_count, coarse), np.float32)
    for fine_row in range(fine_count):
        numerator = (2 * fine_row + 1) * coarse - fine_count
        denominator = 2 * fine_count
        lower_node = min(max(numerator // denominator, 0), coarse - 2)
        fraction = min(max((numerator - lower_node * denominator) / denominator, 0.0), 1.0)
        weights[fine_row, lower_node] += 1.0 - fraction
        weights[fine_row, lower_node + 1] += fraction
    return weights


def azimuth_weights(coarse, fine_count):
    weights = np.zeros((fine_count, coarse), np.float32)
    for fine_column in range(fine_count):
        numerator = fine_column * coarse
        lower_node = numerator // fine_count
        fraction = (numerator - lower_node * fine_count) / fine_count
        weights[fine_column, lower_node] += 1.0 - fraction
        weights[fine_column, (lower_node + 1) % coarse] += fraction
    return weights


def upsample(values):
    leading = values.shape[:-1]
    grid_values = values.reshape(leading + (THETA, PHI))
    polar_table = jnp.asarray(polar_weights(THETA, FINE_THETA), dtype=values.dtype)
    azimuth_table = jnp.asarray(azimuth_weights(PHI, FINE_PHI), dtype=values.dtype)
    refined = jnp.einsum(
        "ia,rvab,jb->rvij", polar_table, grid_values, azimuth_table, precision=lax.Precision.HIGHEST
    )
    return refined.reshape(leading + (FINE_THETA * FINE_PHI,))


def blob_velocity(targets, sources, forcing, blob_size):
    deltas = targets[:, :, None] - sources[:, None, :]
    squared = jnp.sum(deltas * deltas, axis=0)
    inverse = lax.rsqrt(squared + blob_size)
    inverse_cube = inverse * inverse * inverse
    projected = jnp.sum(deltas * forcing[:, None, :], axis=0)
    direct = jnp.sum(
        ((squared + 2.0 * blob_size) * inverse_cube)[None] * forcing[:, None, :], axis=2
    )
    outer_term = jnp.sum((projected * inverse_cube)[None] * deltas, axis=2)
    return STOKES_FACTOR * (direct + outer_term)


def largest_divisor(piece_count, ceiling):
    return max(
        (
            factor
            for factor in range(1, max(1, min(ceiling, piece_count)) + 1)
            if piece_count % factor == 0
        )
    )


def far_blocks(targets, source_spots, forcing):
    piece_count = source_spots.shape[1] // NODES
    per_step = largest_divisor(piece_count, (1 << 21) // (targets.shape[1] * NODES))
    block_width = per_step * NODES
    step_count = piece_count // per_step
    spot_blocks = source_spots.reshape(3, step_count, block_width).transpose(1, 0, 2)
    force_blocks = forcing.reshape(3, step_count, block_width).transpose(1, 0, 2)

    def advance(accumulated, blocks):
        return (accumulated + blob_velocity(targets, blocks[0], blocks[1], FAR_BLOB), None)

    result, unused = lax.scan(
        advance, jnp.zeros(targets.shape, jnp.float32), (spot_blocks, force_blocks)
    )
    return result


def near_groups(aimed_nodes, patch_blocks):
    slot_total = aimed_nodes.shape[0]
    group_size = largest_divisor(slot_total, 16)

    def one_entry(target_nodes, patch_values):
        return blob_velocity(target_nodes, patch_values[:3], patch_values[3:], NEAR_BLOB)

    def one_group(blocks):
        return jax.vmap(one_entry)(blocks[0], blocks[1])

    shaped_targets = aimed_nodes.reshape(
        (slot_total // group_size, group_size) + aimed_nodes.shape[1:]
    )
    shaped_patches = patch_blocks.reshape(
        (slot_total // group_size, group_size) + patch_blocks.shape[1:]
    )
    return lax.map(one_group, (shaped_targets, shaped_patches)).reshape(
        (slot_total,) + aimed_nodes.shape[1:]
    )


def zone_nodes(positions, labels, zone_rows, local_count):
    vesicle = jnp.clip(labels[0], 0, local_count - 1)
    region = jnp.clip(labels[1], 0, zone_rows.shape[0] - 1)
    node_index = vesicle[:, None] * NODES + zone_rows[region]
    picked = jnp.take(positions, node_index.reshape(-1), axis=1).reshape(
        3, node_index.shape[0], node_index.shape[1]
    )
    return jnp.transpose(picked, (1, 0, 2))


def lookup_small(values, queries):
    matches = queries[:, None] == jnp.arange(values.shape[0], dtype=jnp.int32)[None, :]
    return jnp.sum(jnp.where(matches, values[None, :], 0), axis=1)


def on_device(
    positions, forces, owner_map, near_target, near_source, near_patch, patch_rows, zone_rows
):
    shard_width = positions.shape[1]
    local_count = shard_width // NODES
    zone_width = zone_rows.shape[1]
    devices = lax.axis_size(("blk", "tgt"))
    pair_count = near_target.shape[0]
    capacity = max(2, 2 * pair_count // devices)
    slot_count = devices * capacity
    velocity = far_blocks(
        positions,
        lax.all_gather(positions, ("blk", "tgt"), axis=1, tiled=True),
        lax.all_gather(forces, ("blk", "tgt"), axis=1, tiled=True),
    )
    here = lax.axis_index(("blk", "tgt"))
    target_slot = lookup_small(owner_map, near_target)
    source_slot = lookup_small(owner_map, near_source)
    destination = target_slot // local_count
    target_local = target_slot - destination * local_count
    source_local = source_slot - here * local_count
    chosen = (destination[:, None] == jnp.arange(devices, dtype=jnp.int32)[None, :]).astype(
        jnp.int32
    )
    earlier = jnp.cumsum(chosen, axis=0) - chosen
    rank_within = jnp.sum(chosen * earlier, axis=1)
    send_slot = destination * capacity + rank_within
    stacked = jnp.concatenate([positions, forces], axis=0).reshape(6, local_count, NODES)
    refined = upsample(stacked)
    refined = jnp.concatenate([refined[:3], refined[3:] * (NODES / FINE)], axis=0)
    flat_fine = refined.reshape(6, local_count * FINE)
    fine_columns = (source_local[:, None] * FINE + patch_rows[near_patch]).reshape(-1)
    patches = jnp.take(flat_fine, fine_columns, axis=1).reshape(6, pair_count, patch_rows.shape[1])
    labels = jnp.zeros((2, slot_count), jnp.int32).at[0].set(-1)
    labels = (
        labels.at[:, send_slot]
        .set(jnp.stack([target_local, near_patch]))
        .reshape(2, devices, capacity)
    )
    outgoing = (
        jnp.zeros((6, slot_count, patch_rows.shape[1]), jnp.float32).at[:, send_slot].set(patches)
    )
    outgoing = outgoing.reshape(6, devices, capacity, patch_rows.shape[1])
    patch_part = lax.all_to_all(outgoing, ("blk", "tgt"), split_axis=1, concat_axis=1, tiled=True)
    label_part = lax.all_to_all(labels, ("blk", "tgt"), split_axis=1, concat_axis=1, tiled=True)
    width_here = patch_part.shape[2]
    total_slots = devices * width_here
    flat_labels = label_part.reshape(2, total_slots)
    aimed_nodes = zone_nodes(positions, flat_labels, zone_rows, local_count)
    patch_blocks = jnp.transpose(patch_part.reshape(6, total_slots, patch_part.shape[3]), (1, 0, 2))
    results = near_groups(aimed_nodes, patch_blocks)
    results = jnp.transpose(results, (1, 0, 2)).reshape(3, devices, width_here, zone_width)
    owner_labels = label_part.reshape(2, slot_count)
    landing = results.reshape(3, slot_count, zone_width)
    valid = owner_labels[0] >= 0
    landing_vesicle = jnp.clip(owner_labels[0], 0, local_count - 1)
    landing_region = jnp.clip(owner_labels[1], 0, zone_rows.shape[0] - 1)
    landing_index = landing_vesicle[:, None] * NODES + zone_rows[landing_region]
    masked = jnp.where(valid[None, :, None], landing, 0.0)
    patch_velocity = (
        jnp.zeros((3, shard_width), jnp.float32)
        .at[:, landing_index.reshape(-1)]
        .add(masked.reshape(3, -1))
    )
    return (velocity, patch_velocity)


def solution(mesh):
    in_specs = (
        P(None, ("groups", "blk", "tgt")),
        P(None, ("groups", "blk", "tgt")),
        P("groups"),
        P(("groups", "blk", "tgt")),
        P(("groups", "blk", "tgt")),
        P(("groups", "blk", "tgt")),
        P(),
        P(),
    )
    out_specs = (P(None, ("groups", "blk", "tgt")), P(None, ("groups", "blk", "tgt")))
    return jax.shard_map(
        on_device, mesh=mesh, in_specs=in_specs, out_specs=out_specs, check_vma=False
    )
```

profile of v0, /device:TPU:0, one launch (start us, length us, event | category | flops | bytes accessed | tf_op | source)
XLA Modules:
  0.0 611.8 jit_solution(6229454676271197718)
XLA Ops:
  3.7 0.9 scatter_fusion
  5.4 7.4 %all-to-all-start = ((s32[2,16,16]{2,0,1:T(2,128)}), s32[2,16,16]{2,0,1:T(2,128)S(1)}, u32[]{:S(2)}, u32[]{:S(2)}) async-start(s32[2,16,16]{2,0,1:T(2,128)} %copy.58), calls=%async_computation | async-start | bytes 32768 | tf_op jit(solution)/shard_map/all_to_all | solution.py:176
  16.4 1.0 convolution_bitcast_fusion
  18.2 108.2 %gather_fusion.3 = f32[32768,6]{1,0:T(8,128)} fusion(f32[6,2664]{0,1:T(8,128)S(1)} %bitcast.79, s32[32768]{0:T(1024)S(1)} %broadcast_clamp_fusion), kind=kCustom, calls=%fused_computation.3 | custom fusion | bytes 1703936 | tf_op jit(solution)/shard_map/jit(_take)/gather | solution.py:164
  126.4 10.0 %copy.62 = f32[6,128,256]{2,0,1:T(8,128)} copy(f32[6,128,256]{0,2,1:T(8,128)} %bitcast.80) | data formatting | bytes 1572864 | tf_op jit(solution)/shard_map/jit(_take)/gather | solution.py:164
  136.4 22.0 %all-gather = f32[16,312,3]{1,2,0:T(4,128)S(1)} all-gather(f32[1,312,3]{1,2,0:T(4,128)S(1)} %bitcast.98), channel_id=1, replica_groups=mesh['groups'=2,'blk'=4,'tgt'=4] {'blk','tgt'}, dimensions={0}, use_global_device_ids=true | all-gather | bytes 63648 | tf_op jit(solution)/shard_map/all_gather | solution.py:144
  158.5 17.9 %all-gather.1 = f32[16,312,3]{1,2,0:T(4,128)S(1)} all-gather(f32[1,312,3]{1,2,0:T(4,128)S(1)} %bitcast.99), channel_id=1, replica_groups=mesh['groups'=2,'blk'=4,'tgt'=4] {'blk','tgt'}, dimensions={0}, use_global_device_ids=true | all-gather | bytes 63648 | tf_op jit(solution)/shard_map/all_gather | solution.py:145
  176.6 8.1 %fusion.5 = (f32[312,4992]{1,0:T(8,128)}, f32[312,4992]{1,0:T(8,128)}) fusion(f32[3,4992]{1,0:T(4,128)S(1)} %bitcast.90, f32[3,4992]{1,0:T(4,128)S(1)} %bitcast.88, f32[3,312]{1,0:T(4,128)S(1)} %copy-done.5), kind=kLoop, calls=%fused_computation.25 | loop fusion | flops 20247552 | bytes 12583584 | tf_op jit(solution)/shard_map/while/body/eval_jaxpr/reduce_sum | solution.py:61
  184.7 8.6 %fusion.7 = (f32[312,4992]{1,0:T(8,128)}, f32[312,4992]{1,0:T(8,128)S(1)}) fusion(f32[312,4992]{1,0:T(8,128)} %get-tuple-element.72, f32[312,4992]{1,0:T(8,128)} %get-tuple-element.73), kind=kLoop, calls=%fused_computation.31 | loop fusion | flops 9345024 | bytes 24920064 | tf_op jit(solution)/shard_map/while/body/eval_jaxpr/mul | solution.py:65
  193.2 5.2 fusion.6
  198.5 1.8 multiply_reduce_fusion.1
  201.3 4.3 scatter_fusion.1
  205.7 1.6 copy.63
  207.3 3.9 all-to-all-start.1
  212.5 108.2 %gather_fusion.1 = f32[32768,3]{1,0:T(8,128)} fusion(f32[3,312]{0,1:T(8,128)S(1)} %copy.59, s32[32768]{0:T(1024)S(1)} %broadcast_clamp_fusion.1), kind=kCustom, calls=%fused_computation.1 | custom fusion | bytes 917504 | tf_op jit(solution)/shard_map/jit(_take)/gather | solution.py:121
  320.8 11.9 %select_bitcast_fusion = f32[256,3,128]{1,2,0:T(8,128)} fusion(f32[3,256,128]{0,2,1:T(8,128)} %bitcast.81, pred[256,128]{1,0:T(8,128)(4,1)S(1)} %get-tuple-element.86), kind=kLoop, calls=%fused_computation.28 | loop fusion | flops 98304 | bytes 819200 | tf_op jit(solution)/shard_map/transpose | solution.py:124
  332.7 9.5 %copy.60 = f32[256,3,128]{2,1,0:T(4,128)S(1)} copy(f32[256,3,128]{1,2,0:T(8,128)} %select_bitcast_fusion) | data formatting | bytes 786432 | tf_op jit(solution)/shard_map/transpose | solution.py:124
  342.3 85.8 %while.3 = (s32[]{:T(128)}, f32[16,16,3,128]{3,2,1,0:T(4,128)S(1)}, f32[16,16,3,128]{3,2,1,0:T(4,128)S(1)}, f32[16,16,6,256]{3,1,2,0:T(8,128)S(1)}, s32[]{:T(128)}) while((s32[]{:T(128)}, f32[16,16,3,128]{3,2,1,0:T(4,128)S(1)}, f32[16,16,3,128]{3,2,1,0:T(4,128)S(1)}, f32[16,16,6,256]{3,1,2,0:T(8,128)S(1)}, s32[]{:T(128)}) %tuple.55), condition=%wide.region_15.16_spmd, body=%wide.region_10.15_spmd.sunk | while | flops 17825792 | bytes 17809480 | solution.py:112
  342.4 1.7 fusion.25
  344.8 1.9 fusion.27
  346.6 0.9 multiply_reduce_fusion.4
  347.8 1.7 fusion.25
  350.2 1.9 fusion.27
  352.0 0.9 multiply_reduce_fusion.4
  353.2 1.7 fusion.25
  355.5 1.9 fusion.27
  357.4 0.9 multiply_reduce_fusion.4
  358.5 1.7 fusion.25
  360.9 1.9 fusion.27
  362.7 0.9 multiply_reduce_fusion.4
  363.9 1.7 fusion.25
  366.3 1.9 fusion.27
  368.1 0.9 multiply_reduce_fusion.4
  369.3 1.7 fusion.25
  371.6 1.9 fusion.27
  373.5 0.9 multiply_reduce_fusion.4
  374.6 1.7 fusion.25
  377.0 1.9 fusion.27
  378.8 0.9 multiply_reduce_fusion.4
  380.0 1.7 fusion.25
  382.3 1.9 fusion.27
  384.2 0.9 multiply_reduce_fusion.4
  385.4 1.7 fusion.25
  387.7 1.9 fusion.27
  389.6 0.9 multiply_reduce_fusion.4
  390.7 1.7 fusion.25
  393.1 1.9 fusion.27
  394.9 0.9 multiply_reduce_fusion.4
  396.1 1.7 fusion.25
  398.4 1.9 fusion.27
  401.4 1.7 fusion.25
  403.8 1.9 fusion.27
  406.8 1.7 fusion.25
  409.2 1.9 fusion.27
  412.2 1.7 fusion.25
  414.5 1.9 fusion.27
  417.5 1.7 fusion.25
  419.9 1.9 fusion.27
  421.8 0.9 multiply_reduce_fusion.4
  422.9 1.7 fusion.25
  425.3 1.9 fusion.27
  427.1 0.9 multiply_reduce_fusion.4
  428.5 8.3 %copy.66 = f32[3,256,128]{0,2,1:T(8,128)} copy(f32[3,256,128]{2,0,1:T(4,128)S(1)} %bitcast.86) | data formatting | bytes 786432 | tf_op jit(solution)/shard_map/jit(_where)/select_n | solution.py:190
  436.8 174.3 %scatter_custom_fusion.2 = f32[3,312]{0,1:T(8,128)S(1)} fusion(s32[32768]{0:T(1024)S(1)} %bitcast.94, f32[32768,3]{1,0:T(8,128)} %bitcast.82, f32[]{:T(128)} %constant.134.clone.1), kind=kCustom, calls=%fused_computation.42 | custom fusion | flops 98304 | bytes 4256 | tf_op jit(solution)/shard_map/scatter-add | solution.py:194
  (164 shorter events, 27.6 us)
Async XLA Ops:
  0.6 12.8 %copy-start = (s32[32,256]{1,0:T(8,128)S(1)}, s32[32,256]{1,0:T(8,128)}, u32[]{:S(2)}) copy-start(s32[32,256]{1,0:T(8,128)} %param.20) | copy-start | bytes 98308
  5.4 201.9 %all-to-all-start = ((s32[2,16,16]{2,0,1:T(2,128)}), s32[2,16,16]{2,0,1:T(2,128)S(1)}, u32[]{:S(2)}, u32[]{:S(2)}) async-start(s32[2,16,16]{2,0,1:T(2,128)} %copy.58), calls=%async_computation | async-start | bytes 32768 | tf_op jit(solution)/shard_map/all_to_all | solution.py:176
  126.4 10.0 %copy-start.5 = (f32[3,312]{1,0:T(4,128)S(1)}, f32[3,312]{1,0:T(4,128)}, u32[]{:S(2)}) copy-start(f32[3,312]{1,0:T(4,128)} %param.14) | copy-start | bytes 11236
  126.4 32.1 %copy-start.6 = (f32[3,312]{1,0:T(4,128)S(1)}, f32[3,312]{1,0:T(4,128)}, u32[]{:S(2)}) copy-start(f32[3,312]{1,0:T(4,128)} %param.15) | copy-start | bytes 11236
  193.2 7.0 %copy-start.3 = (f32[6,128,256]{2,0,1:T(8,128)S(1)}, f32[6,128,256]{2,0,1:T(8,128)}, u32[]{:S(2)}) copy-start(f32[6,128,256]{2,0,1:T(8,128)} %copy.62) | copy-start | bytes 2359300
  200.4 11.1 %copy-start.2 = (s32[32,128]{1,0:T(8,128)S(1)}, s32[32,128]{1,0:T(8,128)}, u32[]{:S(2)}) copy-start(s32[32,128]{1,0:T(8,128)} %param.21) | copy-start | bytes 49156
  207.3 134.9 %all-to-all-start.1 = ((f32[6,16,16,256]{3,2,0,1:T(8,128)}), f32[6,16,16,256]{3,2,0,1:T(8,128)S(1)}, u32[]{:S(2)}, u32[]{:S(2)}) async-start(f32[6,16,16,256]{3,2,0,1:T(8,128)} %copy.63), calls=%async_computation.1 | async-start | bytes 3145728 | tf_op jit(solution)/shard_map/all_to_all | solution.py:175
  332.6 9.6 %copy-start.4 = (f32[16,16,3,128]{3,2,1,0:T(4,128)S(1)}, f32[16,16,3,128]{3,2,1,0:T(4,128)}, u32[]{:S(2)}) copy-start(f32[16,16,3,128]{3,2,1,0:T(4,128)} %custom-call.8) | copy-start | bytes 1179652
  428.5 183.3 %copy-start.1 = (s32[32,256]{1,0:T(8,128)S(1)}, s32[32,256]{1,0:T(8,128)}, u32[]{:S(2)}) copy-start(s32[32,256]{1,0:T(8,128)} %param.20) | copy-start | bytes 98308
where the time goes:
time: 612 us
  other arithmetic  297 us (49%)
  local copies, waits for them, and re-layouts  259 us (42%)
  blocking collectives  39.8 us (7%)
  starting transfers between devices  11.3 us (2%)
    scatter-add x1, other arithmetic, on_device(): patch_velocity = jnp.zeros((3, shard_width), jnp.float32).at[:, landing_i...  174 us
    gather x2, local copies, waits for them, and re-layouts, on_device(): jnp.take(flat_fine, fine_columns, axis=1)  118 us
    gather x1, local copies, waits for them, and re-layouts, zone_nodes(): jnp.take(positions, node_index.reshape(-1), axis=1)  108 us
    reduce_sum x17, other arithmetic, blob_velocity(): projected = jnp.sum(deltas * forcing[:, None, :], axis=0)  36 us
    reduce_sum x17, other arithmetic, blob_velocity(): outer_term = jnp.sum((projected * inverse_cube)[None] * deltas, axis=2)  34.9 us
    all_gather x1, blocking collectives, on_device(): lax.all_gather(positions, ('blk', 'tgt'), axis=1, tiled=True)  22 us
    mul x17, other arithmetic, blob_velocity(): outer_term = jnp.sum((projected * inverse_cube)[None] * deltas, axis=2)  18.2 us
    all_gather x1, blocking collectives, on_device(): lax.all_gather(forces, ('blk', 'tgt'), axis=1, tiled=True)  17.9 us
  transfers between devices with their start and end apart: 2, of which 0 were waited for; matrix products, arithmetic and copies ran while one was open for 47% of the time, Pallas kernels for 0%

commit v1 on v0

v1 whole, which is shorter than its diff:
```python
import functools
import math

import jax
import jax.numpy as jnp
import numpy as np
from jax import lax
from jax.experimental import pallas as pl
from jax.experimental.pallas import tpu as pltpu
from jax.sharding import PartitionSpec as P

THETA = 13
PHI = 24
FINE_THETA = 37
FINE_PHI = 72
NODES = 312
FINE = 2664
LANES = 128
WIDE = 384
SIDE = 16
ROW = FINE_PHI + SIDE

FAR_BLOB = 0.09
NEAR_BLOB = 0.0025
STOKES_FACTOR = 1.0 / (8.0 * math.pi)


def polar_taps():
    taps = []
    for fine_row in range(FINE_THETA):
        numerator = (2 * fine_row + 1) * THETA - FINE_THETA
        denominator = 2 * FINE_THETA
        lower_node = min(max(numerator // denominator, 0), THETA - 2)
        fraction = min(max((numerator - lower_node * denominator) / denominator, 0.0), 1.0)
        taps.append((lower_node, np.float32(1.0 - fraction), np.float32(fraction)))
    return taps


def pair_terms(x, y, f, blob, sums):
    d = [x[k] - y[k] for k in range(3)]
    squared = d[0] * d[0] + d[1] * d[1] + d[2] * d[2] + blob
    inverse = lax.rsqrt(squared)
    cube = inverse * inverse * inverse
    direct = inverse + blob * cube
    outer = (d[0] * f[0] + d[1] * f[1] + d[2] * f[2]) * cube
    return [sums[k] + (direct * f[k] + outer * d[k]) for k in range(3)]


def split3(value):
    high = value.astype(jnp.bfloat16)
    rest = value - high.astype(jnp.float32)
    middle = rest.astype(jnp.bfloat16)
    low = (rest - middle.astype(jnp.float32)).astype(jnp.bfloat16)
    return jnp.concatenate([high, middle, low], axis=0)


def one_hot(zone_row):
    nodes = lax.broadcasted_iota(jnp.int32, (WIDE, LANES), 0)
    return jnp.where(nodes == zone_row, 1.0, 0.0).astype(jnp.bfloat16)


def upsample(column, coarse, fine):
    for k in range(6):
        coarse[k] = jnp.broadcast_to(column[:, k : k + 1], (WIDE, LANES))
    taps = polar_taps()

    def one_component(k, carry):
        for row, (lower, low_weight, high_weight) in enumerate(taps):
            here = coarse[k, pl.ds(lower * PHI, PHI), :] * low_weight
            here = here + coarse[k, pl.ds((lower + 1) * PHI, PHI), :] * high_weight
            after = jnp.concatenate([here[1:], here[:1]], axis=0)
            third = np.float32(1.0 / 3.0)
            step = (after - here) * third
            fine[k, pl.ds(row * ROW, PHI, stride=3), :] = here
            fine[k, pl.ds(row * ROW + 1, PHI, stride=3), :] = here + step
            fine[k, pl.ds(row * ROW + 2, PHI, stride=3), :] = after - step
            fine[k, pl.ds(row * ROW + FINE_PHI, SIDE), :] = fine[k, pl.ds(row * ROW, SIDE), :]
        return carry

    lax.fori_loop(0, 6, one_component, 0)


def near_part(entries, patches, devices, target_ref, owner_ref, patch_ref, start_ref, zone_ref,
              blocks, fine, table, landed, partial):
    spots = jnp.concatenate([blocks[:, k, :] for k in range(3)], axis=0)
    spots = split3(spots)
    count = 3 * devices

    def gather_zone(p, carry):
        picked = jnp.dot(
            spots, one_hot(zone_ref[pl.ds(p, 1), :]), preferred_element_type=jnp.float32
        )
        table[p] = (picked[2 * count :] + picked[count : 2 * count]) + picked[:count]
        landed[p] = jnp.zeros((count, LANES), jnp.float32)
        return carry

    lax.fori_loop(0, patches, gather_zone, 0)

    def one_entry(e, carry):
        target = owner_ref[target_ref[e]]
        p = patch_ref[e]
        base = start_ref[p]
        x = [
            jnp.broadcast_to(table[p, pl.ds(k * devices + target, 1), :], (8, LANES))
            for k in range(3)
        ]
        sums = [jnp.zeros((8, LANES), jnp.float32)] * 3
        for row in range(SIDE):
            for half in range(2):
                at = pl.ds(base + row * ROW + half * 8, 8)
                y = [fine[k, at, :] for k in range(3)]
                f = [fine[k + 3, at, :] for k in range(3)]
                sums = pair_terms(x, y, f, NEAR_BLOB, sums)
        for k in range(3):
            at = pl.ds(k * devices + target, 1)
            landed[p, at, :] = landed[p, at, :] + jnp.sum(sums[k], axis=0, keepdims=True)
        return carry

    lax.fori_loop(0, entries, one_entry, 0)

    def scatter_zone(p, total):
        hot = one_hot(zone_ref[pl.ds(p, 1), :])
        moved = lax.dot_general(
            split3(landed[p]), hot, (((1,), (1,)), ((), ())), preferred_element_type=jnp.float32
        )
        return total + ((moved[2 * count :] + moved[count : 2 * count]) + moved[:count])

    total = lax.fori_loop(0, patches, scatter_zone, jnp.zeros((count, WIDE), jnp.float32))
    total = total * np.float32(STOKES_FACTOR * NODES / FINE)
    for k in range(3):
        partial[k] = total[k * devices : (k + 1) * devices, :NODES]


def far_part(devices, blocks, coarse, tails, sums_ref, velocity):
    lane = lax.broadcasted_iota(jnp.int32, (8, LANES), 1)

    def merge(b, carry):
        first = blocks[2 * b, :, pl.ds(2 * LANES, LANES)]
        second = blocks[2 * b + 1, :, pl.ds(2 * LANES, LANES)]
        tails[b] = jnp.where(lane < 64, first, pltpu.roll(second, 64, 1))
        return carry

    lax.fori_loop(0, devices // 2, merge, 0)
    group = 3

    def targets(g, carry):
        starts = [pl.multiple_of(g * (8 * group) + 8 * i, 8) for i in range(group)]
        x = [[coarse[k, pl.ds(s, 8), :] for k in range(3)] for s in starts]

        def sources(b, flat):
            sums = [list(flat[3 * i : 3 * i + 3]) for i in range(group)]
            rows = [
                lambda k, i=i, j=j: blocks[2 * b + i, pl.ds(k, 1), pl.ds(j * LANES, LANES)]
                for i in range(2)
                for j in range(2)
            ] + [lambda k: tails[b, pl.ds(k, 1), :]]
            for read in rows:
                values = [jnp.broadcast_to(read(k), (8, LANES)) for k in range(6)]
                for i in range(group):
                    sums[i] = pair_terms(x[i], values[:3], values[3:], FAR_BLOB, sums[i])
            return tuple(v for s in sums for v in s)

        flat = tuple(jnp.zeros((8, LANES), jnp.float32) for _ in range(3 * group))
        flat = lax.fori_loop(0, devices // 2, sources, flat)
        for i in range(group):
            for k in range(3):
                sums_ref[k, pl.ds(starts[i], 8), :] = flat[3 * i + k]
        return carry

    lax.fori_loop(0, NODES // (8 * group), targets, 0)
    ones = jnp.ones((8, LANES), jnp.float32)
    for k in range(3):
        total = lax.dot_general(
            ones, sums_ref[k], (((1,), (1,)), ((), ())),
            precision=lax.Precision.HIGHEST, preferred_element_type=jnp.float32,
        )
        velocity[k : k + 1, :] = total[:1] * np.float32(STOKES_FACTOR)


def interactions(entries, patches, devices, target_ref, owner_ref, patch_ref, start_ref, zone_ref,
                 own_ref, blocks, velocity, partial, coarse, fine, table, landed, tails, sums_ref):
    upsample(own_ref[...].T, coarse, fine)
    near_part(entries, patches, devices, target_ref, owner_ref, patch_ref, start_ref, zone_ref,
              blocks, fine, table, landed, partial)
    far_part(devices, blocks, coarse, tails, sums_ref, velocity)


def patch_starts(patch_rows):
    polar = jnp.min(patch_rows // FINE_PHI, axis=1)
    around = patch_rows % FINE_PHI
    lowest = jnp.min(around, axis=1)
    wrapped = jnp.max(around, axis=1) - lowest >= SIDE
    late = jnp.min(jnp.where(around >= FINE_PHI // 2, around, FINE_PHI), axis=1)
    return polar * ROW + jnp.where(wrapped, late, lowest)


def on_device(
    positions, forces, owner_map, near_target, near_source, near_patch, patch_rows, zone_rows
):
    devices = lax.axis_size(("blk", "tgt"))
    entries = near_target.shape[0]
    patches = patch_rows.shape[0]
    own = jnp.pad(jnp.concatenate([positions, forces], axis=0), ((0, 2), (0, WIDE - NODES)))
    blocks = lax.all_gather(own, ("blk", "tgt"), axis=0)
    smem = pl.BlockSpec(memory_space=pltpu.SMEM)
    vmem = pl.BlockSpec(memory_space=pltpu.VMEM)
    velocity, partial = pl.pallas_call(
        functools.partial(interactions, entries, patches, devices),
        out_shape=(
            jax.ShapeDtypeStruct((3, NODES), jnp.float32),
            jax.ShapeDtypeStruct((3, devices, NODES), jnp.float32),
        ),
        in_specs=[smem] * 4 + [vmem] * 3,
        out_specs=(vmem, vmem),
        scratch_shapes=[
            pltpu.VMEM((6, WIDE, LANES), jnp.float32),
            pltpu.VMEM((6, FINE_THETA * ROW, LANES), jnp.float32),
            pltpu.VMEM((patches, 3 * devices, LANES), jnp.float32),
            pltpu.VMEM((patches, 3 * devices, LANES), jnp.float32),
            pltpu.VMEM((devices // 2, 8, LANES), jnp.float32),
            pltpu.VMEM((3, NODES, LANES), jnp.float32),
        ],
        compiler_params=pltpu.CompilerParams(vmem_limit_bytes=50 * 1024 * 1024),
    )(near_target, owner_map, near_patch, patch_starts(patch_rows), zone_rows, own, blocks)
    patch_velocity = lax.psum_scatter(partial, ("blk", "tgt"), scatter_dimension=1, tiled=True)
    return velocity, patch_velocity.reshape(3, NODES)


def solution(mesh):
    nodes = P(None, ("groups", "blk", "tgt"))
    pairs = P(("groups", "blk", "tgt"))
    in_specs = (nodes, nodes, P("groups"), pairs, pairs, pairs, P(), P())
    return jax.shard_map(
        on_device, mesh=mesh, in_specs=in_specs, out_specs=(nodes, nodes), check_vma=False
    )
```

time: 612 us -> 134 us (0.22)
  other arithmetic: 297 us -> 0.97 us
  local copies, waits for them, and re-layouts: 259 us -> 3.84 us
  Pallas kernels: 0 us -> 46.2 us
  blocking collectives: 39.8 us -> 82.3 us
  starting transfers between devices: 11.3 us -> 0 us
    gather x5 -> x0, local copies, waits for them, and re-layouts: 228 us -> none  [the longest x2 118 us: on_device(): jnp.take(flat_fine, fine_columns, axis=1)]
    scatter-add x1 -> x0, other arithmetic: 174 us -> none  [on_device(): patch_velocity = jnp.zeros((3, shard_width), jnp.float32).at[:, landing_i...]
    reduce_sum x53 -> x0, other arithmetic: 88.8 us -> none  [the longest x17 36 us: blob_velocity(): projected = jnp.sum(deltas * forcing[:, None, :], axis=0)]
    unnamed x0 -> x1, blocking collectives: none -> 58.7 us
    pallas_call x0 -> x1, Pallas kernels: none -> 46.2 us  [on_device(): pl.pallas_call(functools.partial(interactions, entries, patches, devices)...]
    mul x20 -> x0, other arithmetic: 18.9 us -> none  [the longest x17 18.2 us: blob_velocity(): outer_term = jnp.sum((projected * inverse_cube)[None] * deltas, axis=2)]
    all_gather x2 -> x1, blocking collectives: 39.8 us -> 23.6 us  [on_device(): blocks = lax.all_gather(own, ('blk', 'tgt'), axis=0)]
    transpose x1 -> x0, other arithmetic: 11.9 us -> none  [zone_nodes(): return jnp.transpose(picked, (1, 0, 2))]
  transfers between devices with their start and end apart: 2 -> 0, of which waited for: 0 -> 0; matrix products, arithmetic and copies ran while one was open for 47% -> 0% of each run, Pallas kernels for 0% -> 0%
where the time goes in v1:
time: 134 us
  blocking collectives  82.3 us (61%)
  Pallas kernels  46.2 us (34%)
  local copies, waits for them, and re-layouts  3.84 us (3%)
    unnamed x1, blocking collectives  58.7 us
    pallas_call x1, Pallas kernels, on_device(): pl.pallas_call(functools.partial(interactions, entries, patches, devices)...  46.2 us
    all_gather x1, blocking collectives, on_device(): blocks = lax.all_gather(own, ('blk', 'tgt'), axis=0)  23.6 us
    unnamed x17, local copies, waits for them, and re-layouts  3.84 us

profile of v1, /device:TPU:0, one launch (start us, length us, event | category | flops | bytes accessed | tf_op | source)
XLA Modules:
  0.0 133.9 jit_solution(10674872135276400392)
XLA Ops:
  0.6 0.0 copy-start.5
  0.6 0.9 fusion
  1.6 0.0 copy-start.4
  1.6 0.0 copy-done.5
  1.6 0.7 copy-done.4
  2.3 0.0 copy-start
  2.3 23.6 %all-gather = f32[128,384]{1,0:T(8,128)S(1)} all-gather(f32[8,384]{1,0:T(8,128)S(1)} %select_maximum_fusion.own_ref), channel_id=2, replica_groups=mesh['groups'=2,'blk'=4,'tgt'=4] {'blk','tgt'}, dimensions={0}, use_global_device_ids=true | all-gather | bytes 208896 | tf_op jit(solution)/shard_map/all_gather | solution.py:204
  25.9 0.0 copy-start.1
  25.9 0.0 copy-start.2
  25.9 0.0 copy-start.3
  25.9 0.0 copy-done
  25.9 0.6 copy-done.1
  26.6 0.0 copy-done.2
  26.6 0.0 copy-done.3
  26.6 46.2 %shard_map.86 = (f32[3,312]{1,0:T(4,128)}, f32[3,16,312]{2,1,0:T(8,128)S(1)}) custom-call(s32[128]{0:T(128)S(1)} %copy-done.1, s32[16]{0:T(128)S(1)} %copy-done.2, s32[128]{0:T(128)S(1)} %copy-done.3, s32[32]{0:T(128)S(1)} %fusion.5.start_ref, s32[32,128]{1,0:T(8,128)S(1)} %copy-done, f32[8,384]{1,0:T(8,128)S(1)} %select_maximum_fusion.own_ref, ...), custom_call_target="tpu_custom_call" | custom-call | tf_op jit(solution)/shard_map/pallas_call | solution.py:207
  72.8 58.7 %all-reduce.1 = f32[3,16,312]{2,1,0:T(8,128)S(1)} all-reduce(f32[3,16,312]{2,1,0:T(8,128)S(1)} %get-tuple-element.5), channel_id=3, replica_groups=mesh['groups'=2,'blk'=4,'tgt'=4] {'blk','tgt'}, use_global_device_ids=true, to_apply=%region_4.5.clone | all-reduce | flops 14976 | bytes 119808
  131.5 0.0 copy-start.6
  131.5 0.7 copy-done.6
  132.1 0.6 dynamic-slice
  132.7 0.7 constant_dynamic-slice_fusion
  133.4 0.6 copy.13
  (2 shorter events, 0.0 us)
Async XLA Ops:
  0.6 1.0 copy-start.5
  1.6 0.7 copy-start.4
  2.3 23.6 %copy-start = (s32[32,128]{1,0:T(8,128)S(1)}, s32[32,128]{1,0:T(8,128)}, u32[]{:S(2)}) copy-start(s32[32,128]{1,0:T(8,128)} %zone_ref.1) | copy-start | bytes 49156
  25.9 0.7 copy-start.1
  25.9 0.7 copy-start.2
  25.9 0.7 copy-start.3
  131.5 0.7 copy-start.6

commit v2 on v1

--- a/solution.py
+++ b/solution.py
@@ -23,6 +23,7 @@
 FAR_BLOB = 0.09
 NEAR_BLOB = 0.0025
 STOKES_FACTOR = 1.0 / (8.0 * math.pi)
+MESH = pl.DeviceIdType.MESH
 
 
 def polar_taps():
@@ -128,7 +129,7 @@
     total = lax.fori_loop(0, patches, scatter_zone, jnp.zeros((count, WIDE), jnp.float32))
     total = total * np.float32(STOKES_FACTOR * NODES / FINE)
     for k in range(3):
-        partial[k] = total[k * devices : (k + 1) * devices, :NODES]
+        partial[:, k, :] = total[k * devices : (k + 1) * devices]
 
 
 def far_part(devices, blocks, coarse, tails, sums_ref, velocity):
@@ -177,12 +178,87 @@
         velocity[k : k + 1, :] = total[:1] * np.float32(STOKES_FACTOR)
 
 
-def interactions(entries, patches, devices, target_ref, owner_ref, patch_ref, start_ref, zone_ref,
-                 own_ref, blocks, velocity, partial, coarse, fine, table, landed, tails, sums_ref):
+def near_kernel(entries, patches, devices, target_ref, owner_ref, patch_ref, start_ref, zone_ref,
+                own_ref, blocks, partial, coarse, fine, table, landed):
     upsample(own_ref[...].T, coarse, fine)
     near_part(entries, patches, devices, target_ref, owner_ref, patch_ref, start_ref, zone_ref,
               blocks, fine, table, landed, partial)
+
+
+def greet(me, devices, inner):
+    barrier = pltpu.get_barrier_semaphore()
+
+    def signal(i, carry):
+        pl.semaphore_signal(
+            barrier, inc=1, device_id=address(me, i, devices, inner), device_id_type=MESH
+        )
+        return carry
+
+    lax.fori_loop(1, devices, signal, 0)
+    pl.semaphore_wait(barrier, devices - 1)
+
+
+def address(me, step, devices, inner):
+    peer = lax.rem(me + step, devices)
+    return {"blk": peer // inner, "tgt": lax.rem(peer, inner)}
+
+
+def gather_kernel(devices, inner, own_ref, blocks, send_sem, recv_sem):
+    me = lax.axis_index("blk") * inner + lax.axis_index("tgt")
+
+    def copy(step, slot):
+        return pltpu.make_async_remote_copy(
+            src_ref=own_ref, dst_ref=blocks.at[slot], send_sem=send_sem.at[step],
+            recv_sem=recv_sem.at[slot], device_id=address(me, step, devices, inner),
+            device_id_type=MESH,
+        )
+
+    greet(me, devices, inner)
+
+    def start(step, carry):
+        copy(step, me).start()
+        return carry
+
+    lax.fori_loop(1, devices, start, 0)
+    blocks[me] = own_ref[...]
+
+    def finish(step, carry):
+        copy(step, lax.rem(me + devices - step, devices)).wait()
+        return carry
+
+    lax.fori_loop(1, devices, finish, 0)
+
+
+def exchange_kernel(devices, inner, own_ref, blocks, partial, velocity, patch_velocity,
+                    coarse, tails, sums_ref, landing, send_sem, recv_sem):
+    me = lax.axis_index("blk") * inner + lax.axis_index("tgt")
+
+    def copy(step, slot):
+        return pltpu.make_async_remote_copy(
+            src_ref=partial.at[lax.rem(me + step, devices)], dst_ref=landing.at[slot],
+            send_sem=send_sem.at[step], recv_sem=recv_sem.at[slot],
+            device_id=address(me, step, devices, inner), device_id_type=MESH,
+        )
+
+    greet(me, devices, inner)
+
+    def start(step, carry):
+        copy(step, me).start()
+        return carry
+
+    lax.fori_loop(1, devices, start, 0)
+    column = own_ref[...].T
+    for k in range(3):
+        coarse[k] = jnp.broadcast_to(column[:, k : k + 1], (WIDE, LANES))
     far_part(devices, blocks, coarse, tails, sums_ref, velocity)
+
+    def finish(step, total):
+        slot = lax.rem(me + devices - step, devices)
+        copy(step, slot).wait()
+        return total + landing[slot]
+
+    total = lax.fori_loop(1, devices, finish, partial[me])
+    patch_velocity[...] = total[:3, :NODES]
 
 
 def patch_starts(patch_rows):
@@ -201,29 +277,48 @@
     entries = near_target.shape[0]
     patches = patch_rows.shape[0]
     own = jnp.pad(jnp.concatenate([positions, forces], axis=0), ((0, 2), (0, WIDE - NODES)))
-    blocks = lax.all_gather(own, ("blk", "tgt"), axis=0)
+    inner = lax.axis_size("tgt")
     smem = pl.BlockSpec(memory_space=pltpu.SMEM)
     vmem = pl.BlockSpec(memory_space=pltpu.VMEM)
-    velocity, partial = pl.pallas_call(
-        functools.partial(interactions, entries, patches, devices),
-        out_shape=(
-            jax.ShapeDtypeStruct((3, NODES), jnp.float32),
-            jax.ShapeDtypeStruct((3, devices, NODES), jnp.float32),
-        ),
+    block_shape = jax.ShapeDtypeStruct((devices, 8, WIDE), jnp.float32)
+    node_shape = jax.ShapeDtypeStruct((3, NODES), jnp.float32)
+    semaphores = [pltpu.SemaphoreType.DMA((devices,))] * 2
+    blocks = pl.pallas_call(
+        functools.partial(gather_kernel, devices, inner),
+        out_shape=block_shape,
+        in_specs=[vmem],
+        out_specs=vmem,
+        scratch_shapes=semaphores,
+        compiler_params=pltpu.CompilerParams(collective_id=0, has_side_effects=True),
+    )(own)
+    partial = pl.pallas_call(
+        functools.partial(near_kernel, entries, patches, devices),
+        out_shape=block_shape,
         in_specs=[smem] * 4 + [vmem] * 3,
-        out_specs=(vmem, vmem),
+        out_specs=vmem,
         scratch_shapes=[
             pltpu.VMEM((6, WIDE, LANES), jnp.float32),
             pltpu.VMEM((6, FINE_THETA * ROW, LANES), jnp.float32),
             pltpu.VMEM((patches, 3 * devices, LANES), jnp.float32),
             pltpu.VMEM((patches, 3 * devices, LANES), jnp.float32),
-            pltpu.VMEM((devices // 2, 8, LANES), jnp.float32),
-            pltpu.VMEM((3, NODES, LANES), jnp.float32),
         ],
         compiler_params=pltpu.CompilerParams(vmem_limit_bytes=50 * 1024 * 1024),
     )(near_target, owner_map, near_patch, patch_starts(patch_rows), zone_rows, own, blocks)
-    patch_velocity = lax.psum_scatter(partial, ("blk", "tgt"), scatter_dimension=1, tiled=True)
-    return velocity, patch_velocity.reshape(3, NODES)
+    return pl.pallas_call(
+        functools.partial(exchange_kernel, devices, inner),
+        out_shape=(node_shape, node_shape),
+        in_specs=[vmem] * 3,
+        out_specs=(vmem, vmem),
+        scratch_shapes=[
+            pltpu.VMEM((3, WIDE, LANES), jnp.float32),
+            pltpu.VMEM((devices // 2, 8, LANES), jnp.float32),
+            pltpu.VMEM((3, NODES, LANES), jnp.float32),
+            pltpu.VMEM((devices, 8, WIDE), jnp.float32),
+        ] + semaphores,
+        compiler_params=pltpu.CompilerParams(
+            collective_id=1, has_side_effects=True, vmem_limit_bytes=50 * 1024 * 1024
+        ),
+    )(own, blocks, partial)
 
 
 def solution(mesh):

time: 134 us -> 69.2 us (0.52)
  blocking collectives: 82.3 us -> 0 us
  Pallas kernels: 46.2 us -> 63.8 us
    unnamed x1 -> x0, blocking collectives: 58.7 us -> none
    all_gather x1 -> x0, blocking collectives: 23.6 us -> none  [on_device(): blocks = lax.all_gather(own, ('blk', 'tgt'), axis=0)]
    pallas_call x1 -> x3, Pallas kernels: 46.2 us -> 63.8 us  [the longest x1 37.6 us: on_device(): pl.pallas_call(functools.partial(near_kernel, entries, patches, devices),...]
    unnamed x17 -> x18, local copies, waits for them, and re-layouts: 3.84 us -> 2.8 us
where the time goes in v2:
time: 69.2 us; the launch traced here: 68.9 us
  Pallas kernels  63.8 us (92%)
  local copies, waits for them, and re-layouts  2.8 us (4%)
  other arithmetic  1.56 us (2%)
  between operations  0.75 us (1%)
    pallas_call x1, Pallas kernels, on_device(): pl.pallas_call(functools.partial(near_kernel, entries, patches, devices),...  37.6 us
    pallas_call x1, Pallas kernels, on_device(): pl.pallas_call(functools.partial(exchange_kernel, devices, inner), out_sh...  14.7 us
    pallas_call x1, Pallas kernels, on_device(): pl.pallas_call(functools.partial(gather_kernel, devices, inner), out_shap...  11.5 us
    unnamed x18, local copies, waits for them, and re-layouts  2.8 us

profile of v2, /device:TPU:0, one launch (start us, length us, event | category | flops | bytes accessed | tf_op | source)
XLA Modules:
  0.0 68.9 jit_solution(1356801019206768077)
XLA Ops:
  0.6 0.0 copy-start.7
  0.6 0.9 %fusion = (s32[32]{0:T(128)S(1)}, s32[32]{0:T(128)S(1)}, s32[32]{0:T(128)S(1)}, s32[32]{0:T(128)S(1)}) fusion(s32[32,256]{1,0:T(8,128)} %param.13), kind=kLoop, calls=%fused_computation.3 | loop fusion | flops 147328 | bytes 33280 | tf_op jit(solution)/shard_map/reduce_min | solution.py:265
  1.6 0.0 copy-start.6
  1.6 0.0 copy-done.7
  1.6 0.7 copy-done.6
  2.3 0.6 select_maximum_fusion.own_ref
  2.9 0.0 copy-start.1
  2.9 0.0 copy-start.2
  2.9 0.0 copy-start.3
  2.9 0.0 copy-start.4
  2.9 0.0 copy-start.5
  2.9 11.5 %shard_map.86.blocks = f32[16,8,384]{2,1,0:T(8,128)} custom-call(f32[8,384]{1,0:T(8,128)} %select_maximum_fusion.own_ref), custom_call_target="tpu_custom_call" | custom-call | tf_op jit(solution)/shard_map/pallas_call | solution.py:286
  14.4 0.0 copy-done.1
  14.5 0.0 copy-done.2
  14.5 0.0 copy-done.3
  14.5 0.0 copy-done.4
  14.5 0.0 copy-done.5
  14.5 0.0 copy-start
  14.5 0.9 %copy-done = f32[16,8,384]{2,1,0:T(8,128)S(1)} copy-done((f32[16,8,384]{2,1,0:T(8,128)S(1)}, f32[16,8,384]{2,1,0:T(8,128)}, u32[]{:S(2)}) %copy-start) | copy-done | bytes 196632
  15.4 37.6 %shard_map.87.partial = f32[16,8,384]{2,1,0:T(8,128)S(1)} custom-call(s32[128]{0:T(128)S(1)} %copy-done.3, s32[16]{0:T(128)S(1)} %copy-done.4, s32[128]{0:T(128)S(1)} %copy-done.5, s32[32]{0:T(128)S(1)} %fusion.5.start_ref, s32[32,128]{1,0:T(8,128)S(1)} %copy-done.2, f32[8,384]{1,0:T(8,128)S(1)} %copy-done.1, f32[16,8,384]{2,1,0:T(8,128)S(1)} %copy-done), custom_call_target="tpu_custom_call" | custom-call | tf_op jit(solution)/shard_map/pallas_call | solution.py:294
  53.0 14.7 %shard_map.88 = (f32[3,312]{1,0:T(4,128)S(1)}, f32[3,312]{1,0:T(4,128)S(1)}) custom-call(f32[8,384]{1,0:T(8,128)S(1)} %copy-done.1, f32[16,8,384]{2,1,0:T(8,128)S(1)} %copy-done, f32[16,8,384]{2,1,0:T(8,128)S(1)} %shard_map.87.partial), custom_call_target="tpu_custom_call" | custom-call | tf_op jit(solution)/shard_map/pallas_call | solution.py:307
  67.8 0.6 copy.11
  68.3 0.6 copy.12
  (1 shorter events, 0.0 us)
Async XLA Ops:
  0.6 1.0 %copy-start.7 = (f32[3,312]{1,0:T(4,128)S(1)}, f32[3,312]{1,0:T(4,128)}, u32[]{:S(2)}) copy-start(f32[3,312]{1,0:T(4,128)} %param.8) | copy-start | bytes 11236
  1.6 0.7 %copy-start.6 = (f32[3,312]{1,0:T(4,128)S(1)}, f32[3,312]{1,0:T(4,128)}, u32[]{:S(2)}) copy-start(f32[3,312]{1,0:T(4,128)} %param.9) | copy-start | bytes 11236
  2.9 11.6 %copy-start.1 = (f32[8,384]{1,0:T(8,128)S(1)}, f32[8,384]{1,0:T(8,128)}, u32[]{:S(2)}) copy-start(f32[8,384]{1,0:T(8,128)} %select_maximum_fusion.own_ref) | copy-start | bytes 36868
  2.9 11.6 %copy-start.2 = (s32[32,128]{1,0:T(8,128)S(1)}, s32[32,128]{1,0:T(8,128)}, u32[]{:S(2)}) copy-start(s32[32,128]{1,0:T(8,128)} %zone_ref.1) | copy-start | bytes 49156
  2.9 11.6 %copy-start.3 = (s32[128]{0:T(128)S(1)}, s32[128]{0:T(128)}, u32[]{:S(2)}) copy-start(s32[128]{0:T(128)} %target_ref.1) | copy-start | bytes 1540
  2.9 11.6 %copy-start.4 = (s32[16]{0:T(128)S(1)}, s32[16]{0:T(128)}, u32[]{:S(2)}) copy-start(s32[16]{0:T(128)} %owner_ref.1) | copy-start | bytes 196
  2.9 11.6 %copy-start.5 = (s32[128]{0:T(128)S(1)}, s32[128]{0:T(128)}, u32[]{:S(2)}) copy-start(s32[128]{0:T(128)} %patch_ref.1) | copy-start | bytes 1540
  14.5 0.9 %copy-start = (f32[16,8,384]{2,1,0:T(8,128)S(1)}, f32[16,8,384]{2,1,0:T(8,128)}, u32[]{:S(2)}) copy-start(f32[16,8,384]{2,1,0:T(8,128)} %shard_map.86.blocks) | copy-start | bytes 589828

commit v3 on v1

--- a/solution.py
+++ b/solution.py
@@ -23,6 +23,7 @@
 FAR_BLOB = 0.09
 NEAR_BLOB = 0.0025
 STOKES_FACTOR = 1.0 / (8.0 * math.pi)
+MESH = pl.DeviceIdType.MESH
 
 
 def polar_taps():
@@ -54,9 +55,11 @@
     return jnp.concatenate([high, middle, low], axis=0)
 
 
-def one_hot(zone_row):
+def zone_tables(patches, zone_ref, hot):
     nodes = lax.broadcasted_iota(jnp.int32, (WIDE, LANES), 0)
-    return jnp.where(nodes == zone_row, 1.0, 0.0).astype(jnp.bfloat16)
+    for p in range(patches):
+        found = nodes == zone_ref[p : p + 1, :]
+        hot[:, p * LANES : (p + 1) * LANES] = jnp.where(found, 1.0, 0.0).astype(jnp.bfloat16)
 
 
 def upsample(column, coarse, fine):
@@ -80,21 +83,21 @@
     lax.fori_loop(0, 6, one_component, 0)
 
 
-def near_part(entries, patches, devices, target_ref, owner_ref, patch_ref, start_ref, zone_ref,
-              blocks, fine, table, landed, partial):
+def near_part(entries, patches, devices, target_ref, owner_ref, patch_ref, start_ref,
+              listed_ref, blocks, fine, hot, table, results, partial):
     spots = jnp.concatenate([blocks[:, k, :] for k in range(3)], axis=0)
     spots = split3(spots)
     count = 3 * devices
-
-    def gather_zone(p, carry):
+    batch = 8
+
+    for first in range(0, patches, batch):
         picked = jnp.dot(
-            spots, one_hot(zone_ref[pl.ds(p, 1), :]), preferred_element_type=jnp.float32
-        )
-        table[p] = (picked[2 * count :] + picked[count : 2 * count]) + picked[:count]
-        landed[p] = jnp.zeros((count, LANES), jnp.float32)
-        return carry
-
-    lax.fori_loop(0, patches, gather_zone, 0)
+            spots, hot[:, first * LANES : (first + batch) * LANES],
+            preferred_element_type=jnp.float32,
+        )
+        picked = (picked[2 * count :] + picked[count : 2 * count]) + picked[:count]
+        for i in range(batch):
+            table[first + i] = picked[:, i * LANES : (i + 1) * LANES]
 
     def one_entry(e, carry):
         target = owner_ref[target_ref[e]]
@@ -112,23 +115,40 @@
                 f = [fine[k + 3, at, :] for k in range(3)]
                 sums = pair_terms(x, y, f, NEAR_BLOB, sums)
         for k in range(3):
-            at = pl.ds(k * devices + target, 1)
-            landed[p, at, :] = landed[p, at, :] + jnp.sum(sums[k], axis=0, keepdims=True)
+            results[k, pl.ds(e, 1), :] = jnp.sum(sums[k], axis=0, keepdims=True)
         return carry
 
     lax.fori_loop(0, entries, one_entry, 0)
 
-    def scatter_zone(p, total):
-        hot = one_hot(zone_ref[pl.ds(p, 1), :])
-        moved = lax.dot_general(
-            split3(landed[p]), hot, (((1,), (1,)), ((), ())), preferred_element_type=jnp.float32
-        )
-        return total + ((moved[2 * count :] + moved[count : 2 * count]) + moved[:count])
-
-    total = lax.fori_loop(0, patches, scatter_zone, jnp.zeros((count, WIDE), jnp.float32))
-    total = total * np.float32(STOKES_FACTOR * NODES / FINE)
+    named = listed_ref[0:1, :]
+    slot = lax.fori_loop(
+        0, devices, lambda v, found: jnp.where(named == v, owner_ref[v], found),
+        jnp.zeros((1, entries), jnp.int32),
+    )
+    slots = lax.broadcasted_iota(jnp.int32, (devices, entries), 0)
+    here = slots == slot
+    region = listed_ref[1:2, :]
+    values = split3(jnp.concatenate([results[k] for k in range(3)], axis=1))
+    total = [jnp.zeros((3 * devices, WIDE), jnp.float32) for _ in range(3)]
+    for first in range(0, patches, batch):
+        chosen = jnp.concatenate(
+            [jnp.where(here & (region == first + i), 1.0, 0.0) for i in range(batch)], axis=0
+        ).astype(jnp.bfloat16)
+        landed = jnp.dot(
+            jnp.concatenate([chosen] * 3, axis=1), values, preferred_element_type=jnp.float32
+        )
+        for k in range(3):
+            mine = landed[:, k * LANES : (k + 1) * LANES]
+            mine = jnp.concatenate(
+                [mine[i * devices : (i + 1) * devices] for i in range(batch)], axis=1
+            )
+            total[k] = total[k] + lax.dot_general(
+                split3(mine), hot[:, first * LANES : (first + batch) * LANES],
+                (((1,), (1,)), ((), ())), preferred_element_type=jnp.float32,
+            )
     for k in range(3):
-        partial[k] = total[k * devices : (k + 1) * devices, :NODES]
+        moved = (total[k][2 * devices :] + total[k][devices : 2 * devices]) + total[k][:devices]
+        partial[:, k, :] = moved * np.float32(STOKES_FACTOR * NODES / FINE)
 
 
 def far_part(devices, blocks, coarse, tails, sums_ref, velocity):
@@ -177,12 +197,76 @@
         velocity[k : k + 1, :] = total[:1] * np.float32(STOKES_FACTOR)
 
 
-def interactions(entries, patches, devices, target_ref, owner_ref, patch_ref, start_ref, zone_ref,
-                 own_ref, blocks, velocity, partial, coarse, fine, table, landed, tails, sums_ref):
+def greet(me, devices, inner):
+    barrier = pltpu.get_barrier_semaphore()
+
+    def signal(i, carry):
+        pl.semaphore_signal(
+            barrier, inc=1, device_id=address(me, i, devices, inner), device_id_type=MESH
+        )
+        return carry
+
+    lax.fori_loop(1, devices, signal, 0)
+    pl.semaphore_wait(barrier, devices - 1)
+
+
+def address(me, step, devices, inner):
+    peer = lax.rem(me + step, devices)
+    return {"blk": peer // inner, "tgt": lax.rem(peer, inner)}
+
+
+def interactions(entries, patches, devices, inner, target_ref, owner_ref, patch_ref, start_ref,
+                 listed_ref, zone_ref, own_ref, velocity, patch_velocity, blocks, coarse, fine, hot,
+                 table, results, partial, landing, tails, sums_ref, sent, arrived, returned, landed):
+    me = lax.axis_index("blk") * inner + lax.axis_index("tgt")
+
+    def spread(step, slot):
+        return pltpu.make_async_remote_copy(
+            src_ref=own_ref, dst_ref=blocks.at[slot], send_sem=sent.at[step],
+            recv_sem=arrived.at[slot], device_id=address(me, step, devices, inner),
+            device_id_type=MESH,
+        )
+
+    def give_back(step, slot):
+        return pltpu.make_async_remote_copy(
+            src_ref=partial.at[lax.rem(me + step, devices)], dst_ref=landing.at[slot],
+            send_sem=returned.at[step], recv_sem=landed.at[slot],
+            device_id=address(me, step, devices, inner), device_id_type=MESH,
+        )
+
+    greet(me, devices, inner)
+
+    def start(step, carry):
+        spread(step, me).start()
+        return carry
+
+    lax.fori_loop(1, devices, start, 0)
+    blocks[me] = own_ref[...]
     upsample(own_ref[...].T, coarse, fine)
-    near_part(entries, patches, devices, target_ref, owner_ref, patch_ref, start_ref, zone_ref,
-              blocks, fine, table, landed, partial)
+    zone_tables(patches, zone_ref, hot)
+
+    def arrive(step, carry):
+        spread(step, lax.rem(me + devices - step, devices)).wait()
+        return carry
+
+    lax.fori_loop(1, devices, arrive, 0)
+    near_part(entries, patches, devices, target_ref, owner_ref, patch_ref, start_ref,
+              listed_ref, blocks, fine, hot, table, results, partial)
+
+    def start_back(step, carry):
+        give_back(step, me).start()
+        return carry
+
+    lax.fori_loop(1, devices, start_back, 0)
     far_part(devices, blocks, coarse, tails, sums_ref, velocity)
+
+    def finish(step, total):
+        slot = lax.rem(me + devices - step, devices)
+        give_back(step, slot).wait()
+        return total + landing[slot]
+
+    total = lax.fori_loop(1, devices, finish, partial[me])
+    patch_velocity[...] = total[:3, :NODES]
 
 
 def patch_starts(patch_rows):
@@ -201,29 +285,32 @@
     entries = near_target.shape[0]
     patches = patch_rows.shape[0]
     own = jnp.pad(jnp.concatenate([positions, forces], axis=0), ((0, 2), (0, WIDE - NODES)))
-    blocks = lax.all_gather(own, ("blk", "tgt"), axis=0)
+    inner = lax.axis_size("tgt")
     smem = pl.BlockSpec(memory_space=pltpu.SMEM)
     vmem = pl.BlockSpec(memory_space=pltpu.VMEM)
-    velocity, partial = pl.pallas_call(
-        functools.partial(interactions, entries, patches, devices),
-        out_shape=(
-            jax.ShapeDtypeStruct((3, NODES), jnp.float32),
-            jax.ShapeDtypeStruct((3, devices, NODES), jnp.float32),
-        ),
+    node_shape = jax.ShapeDtypeStruct((3, NODES), jnp.float32)
+    return pl.pallas_call(
+        functools.partial(interactions, entries, patches, devices, inner),
+        out_shape=(node_shape, node_shape),
         in_specs=[smem] * 4 + [vmem] * 3,
         out_specs=(vmem, vmem),
         scratch_shapes=[
+            pltpu.VMEM((devices, 8, WIDE), jnp.float32),
             pltpu.VMEM((6, WIDE, LANES), jnp.float32),
             pltpu.VMEM((6, FINE_THETA * ROW, LANES), jnp.float32),
+            pltpu.VMEM((WIDE, patches * LANES), jnp.bfloat16),
             pltpu.VMEM((patches, 3 * devices, LANES), jnp.float32),
-            pltpu.VMEM((patches, 3 * devices, LANES), jnp.float32),
+            pltpu.VMEM((3, entries, LANES), jnp.float32),
+            pltpu.VMEM((devices, 8, WIDE), jnp.float32),
+            pltpu.VMEM((devices, 8, WIDE), jnp.float32),
             pltpu.VMEM((devices // 2, 8, LANES), jnp.float32),
             pltpu.VMEM((3, NODES, LANES), jnp.float32),
-        ],
-        compiler_params=pltpu.CompilerParams(vmem_limit_bytes=50 * 1024 * 1024),
-    )(near_target, owner_map, near_patch, patch_starts(patch_rows), zone_rows, own, blocks)
-    patch_velocity = lax.psum_scatter(partial, ("blk", "tgt"), scatter_dimension=1, tiled=True)
-    return velocity, patch_velocity.reshape(3, NODES)
+        ] + [pltpu.SemaphoreType.DMA((devices,))] * 4,
+        compiler_params=pltpu.CompilerParams(
+            collective_id=0, has_side_effects=True, vmem_limit_bytes=50 * 1024 * 1024
+        ),
+    )(near_target, owner_map, near_patch, patch_starts(patch_rows),
+      jnp.stack([near_target, near_patch]), zone_rows, own)
 
 
 def solution(mesh):

time: 134 us -> 52.3 us (0.39)
  blocking collectives: 82.3 us -> 0 us
    unnamed x1 -> x0, blocking collectives: 58.7 us -> none
    all_gather x1 -> x0, blocking collectives: 23.6 us -> none  [on_device(): blocks = lax.all_gather(own, ('blk', 'tgt'), axis=0)]
    unnamed x17 -> x14, local copies, waits for them, and re-layouts: 3.84 us -> 3.15 us
where the time goes in v3:
time: 52.3 us; the launch traced here: 52.1 us
  Pallas kernels  47.2 us (90%)
  local copies, waits for them, and re-layouts  3.15 us (6%)
  other arithmetic  0.98 us (2%)
  between operations  0.69 us (1%)
    pallas_call x1, Pallas kernels, on_device(): pl.pallas_call(functools.partial(interactions, entries, patches, devices,...  47.2 us
    unnamed x14, local copies, waits for them, and re-layouts  3.15 us

profile of v3, /device:TPU:0, one launch (start us, length us, event | category | flops | bytes accessed | tf_op | source)
XLA Modules:
  0.0 52.1 jit_solution(18162135755533494701)
XLA Ops:
  0.6 0.0 copy-start.1
  0.6 0.0 copy-start.2
  0.6 0.6 %copy-done.1 = s32[128]{0:T(128)S(1)} copy-done((s32[128]{0:T(128)S(1)}, s32[128]{0:T(128)}, u32[]{:S(2)}) %copy-start.1) | copy-done | bytes 536
  1.3 0.0 copy-done.2
  1.3 0.0 copy-start.5
  1.3 1.0 %fusion = (s32[32]{0:T(128)S(1)}, s32[32]{0:T(128)S(1)}, s32[32]{0:T(128)S(1)}, s32[32]{0:T(128)S(1)}) fusion(s32[32,256]{1,0:T(8,128)} %param.13), kind=kLoop, calls=%fused_computation.3 | loop fusion | flops 147328 | bytes 33280 | tf_op jit(solution)/shard_map/reduce_min | solution.py:273
  2.3 0.0 copy-start.4
  2.3 0.0 copy-start
  2.3 0.0 copy-done.5
  2.3 0.6 %copy-done.4 = f32[3,312]{1,0:T(4,128)S(1)} copy-done((f32[3,312]{1,0:T(4,128)S(1)}, f32[3,312]{1,0:T(4,128)}, u32[]{:S(2)}) %copy-start.4) | copy-done | bytes 3768
  3.0 0.0 copy-start.3
  3.0 0.0 copy-done
  3.0 0.6 %copy-done.3 = s32[16]{0:T(128)S(1)} copy-done((s32[16]{0:T(128)S(1)}, s32[16]{0:T(128)}, u32[]{:S(2)}) %copy-start.3) | copy-done | bytes 88
  3.6 47.2 %shard_map.86 = (f32[3,312]{1,0:T(4,128)S(1)}, f32[3,312]{1,0:T(4,128)S(1)}) custom-call(s32[128]{0:T(128)S(1)} %copy-done.1, s32[16]{0:T(128)S(1)} %copy-done.3, s32[128]{0:T(128)S(1)} %copy-done.2, s32[32]{0:T(128)S(1)} %fusion.5.start_ref, s32[2,128]{1,0:T(2,128)S(1)} %pad_add_fusion.listed_ref, s32[32,128]{1,0:T(8,128)S(1)} %copy-done, ...), custom_call_target="tpu_custom_call" | custom-call | tf_op jit(solution)/shard_map/pallas_call | solution.py:292
  50.9 0.6 %copy.11 = f32[3,312]{1,0:T(4,128)} copy(f32[3,312]{1,0:T(4,128)S(1)} %get-tuple-element.8) | data formatting | bytes 7488
  51.5 0.6 %copy.12 = f32[3,312]{1,0:T(4,128)} copy(f32[3,312]{1,0:T(4,128)S(1)} %get-tuple-element.9) | data formatting | bytes 7488
  (3 shorter events, 0.0 us)
Async XLA Ops:
  0.6 0.7 %copy-start.1 = (s32[128]{0:T(128)S(1)}, s32[128]{0:T(128)}, u32[]{:S(2)}) copy-start(s32[128]{0:T(128)} %target_ref.1) | copy-start | bytes 1540
  0.6 0.7 %copy-start.2 = (s32[128]{0:T(128)S(1)}, s32[128]{0:T(128)}, u32[]{:S(2)}) copy-start(s32[128]{0:T(128)} %patch_ref.1) | copy-start | bytes 1540
  1.3 1.0 %copy-start.5 = (f32[3,312]{1,0:T(4,128)S(1)}, f32[3,312]{1,0:T(4,128)}, u32[]{:S(2)}) copy-start(f32[3,312]{1,0:T(4,128)} %param.8) | copy-start | bytes 11236
  2.3 0.7 %copy-start.4 = (f32[3,312]{1,0:T(4,128)S(1)}, f32[3,312]{1,0:T(4,128)}, u32[]{:S(2)}) copy-start(f32[3,312]{1,0:T(4,128)} %param.9) | copy-start | bytes 11236
  2.3 0.7 %copy-start = (s32[32,128]{1,0:T(8,128)S(1)}, s32[32,128]{1,0:T(8,128)}, u32[]{:S(2)}) copy-start(s32[32,128]{1,0:T(8,128)} %zone_ref.1) | copy-start | bytes 49156
  3.0 0.7 %copy-start.3 = (s32[16]{0:T(128)S(1)}, s32[16]{0:T(128)}, u32[]{:S(2)}) copy-start(s32[16]{0:T(128)} %owner_ref.1) | copy-start | bytes 196

commit v4 on v3

--- a/solution.py
+++ b/solution.py
@@ -23,6 +23,7 @@
 FAR_BLOB = 0.09
 NEAR_BLOB = 0.0025
 STOKES_FACTOR = 1.0 / (8.0 * math.pi)
+ENTRIES_STEP = 4
 MESH = pl.DeviceIdType.MESH
 
 
@@ -37,12 +38,12 @@
     return taps
 
 
-def pair_terms(x, y, f, blob, sums):
+def pair_terms(x, y, f, sums):
     d = [x[k] - y[k] for k in range(3)]
-    squared = d[0] * d[0] + d[1] * d[1] + d[2] * d[2] + blob
+    squared = d[0] * d[0] + d[1] * d[1] + (d[2] * d[2] + 1.0)
     inverse = lax.rsqrt(squared)
     cube = inverse * inverse * inverse
-    direct = inverse + blob * cube
+    direct = inverse + cube
     outer = (d[0] * f[0] + d[1] * f[1] + d[2] * f[2]) * cube
     return [sums[k] + (direct * f[k] + outer * d[k]) for k in range(3)]
 
@@ -64,7 +65,8 @@
 
 def upsample(column, coarse, fine):
     for k in range(6):
-        coarse[k] = jnp.broadcast_to(column[:, k : k + 1], (WIDE, LANES))
+        scale = np.float32(1.0 / math.sqrt(NEAR_BLOB)) if k < 3 else np.float32(1.0)
+        coarse[k] = jnp.broadcast_to(column[:, k : k + 1] * scale, (WIDE, LANES))
     taps = polar_taps()
 
     def one_component(k, carry):
@@ -86,7 +88,7 @@
 def near_part(entries, patches, devices, target_ref, owner_ref, patch_ref, start_ref,
               listed_ref, blocks, fine, hot, table, results, partial):
     spots = jnp.concatenate([blocks[:, k, :] for k in range(3)], axis=0)
-    spots = split3(spots)
+    spots = split3(spots * np.float32(1.0 / math.sqrt(NEAR_BLOB)))
     count = 3 * devices
     batch = 8
 
@@ -99,35 +101,36 @@
         for i in range(batch):
             table[first + i] = picked[:, i * LANES : (i + 1) * LANES]
 
-    def one_entry(e, carry):
-        target = owner_ref[target_ref[e]]
-        p = patch_ref[e]
-        base = start_ref[p]
-        x = [
-            jnp.broadcast_to(table[p, pl.ds(k * devices + target, 1), :], (8, LANES))
-            for k in range(3)
-        ]
-        sums = [jnp.zeros((8, LANES), jnp.float32)] * 3
-        for row in range(SIDE):
-            for half in range(2):
-                at = pl.ds(base + row * ROW + half * 8, 8)
-                y = [fine[k, at, :] for k in range(3)]
-                f = [fine[k + 3, at, :] for k in range(3)]
-                sums = pair_terms(x, y, f, NEAR_BLOB, sums)
-        for k in range(3):
-            results[k, pl.ds(e, 1), :] = jnp.sum(sums[k], axis=0, keepdims=True)
-        return carry
-
-    lax.fori_loop(0, entries, one_entry, 0)
-
-    named = listed_ref[0:1, :]
+    def some_entries(step, carry):
+        for i in range(ENTRIES_STEP):
+            e = step * ENTRIES_STEP + i
+            target = owner_ref[target_ref[e]]
+            p = patch_ref[e]
+            base = start_ref[p, 0]
+            x = [
+                jnp.broadcast_to(table[p, pl.ds(k * devices + target, 1), :], (8, LANES))
+                for k in range(3)
+            ]
+            sums = [jnp.zeros((8, LANES), jnp.float32)] * 3
+            for row in range(SIDE):
+                for half in range(2):
+                    at = pl.ds(base + row * ROW + half * 8, 8)
+                    y = [fine[k, at, :] for k in range(3)]
+                    f = [fine[k + 3, at, :] for k in range(3)]
+                    sums = pair_terms(x, y, f, sums)
+            for k in range(3):
+                results[k, pl.ds(e, 1), :] = jnp.sum(sums[k], axis=0, keepdims=True)
+        return carry
+
+    lax.fori_loop(0, entries // ENTRIES_STEP, some_entries, 0)
+
+    named, region = listed_ref[0][...], listed_ref[1][...]
     slot = lax.fori_loop(
         0, devices, lambda v, found: jnp.where(named == v, owner_ref[v], found),
         jnp.zeros((1, entries), jnp.int32),
     )
     slots = lax.broadcasted_iota(jnp.int32, (devices, entries), 0)
     here = slots == slot
-    region = listed_ref[1:2, :]
     values = split3(jnp.concatenate([results[k] for k in range(3)], axis=1))
     total = [jnp.zeros((3 * devices, WIDE), jnp.float32) for _ in range(3)]
     for first in range(0, patches, batch):
@@ -148,11 +151,22 @@
             )
     for k in range(3):
         moved = (total[k][2 * devices :] + total[k][devices : 2 * devices]) + total[k][:devices]
-        partial[:, k, :] = moved * np.float32(STOKES_FACTOR * NODES / FINE)
-
-
-def far_part(devices, blocks, coarse, tails, sums_ref, velocity):
+        partial[:, k, :] = moved * np.float32(STOKES_FACTOR * NODES / FINE / math.sqrt(NEAR_BLOB))
+
+
+def far_part(devices, own_ref, blocks, coarse, tails, sums_ref, velocity):
     lane = lax.broadcasted_iota(jnp.int32, (8, LANES), 1)
+    row = lax.broadcasted_iota(jnp.int32, (8, WIDE), 0)
+    scale = jnp.where(row < 3, np.float32(1.0 / math.sqrt(FAR_BLOB)), np.float32(1.0))
+    column = (own_ref[...] * scale).T
+    for k in range(3):
+        coarse[k] = jnp.broadcast_to(column[:, k : k + 1], (WIDE, LANES))
+
+    def shrink(b, carry):
+        blocks[b] = blocks[b] * scale
+        return carry
+
+    lax.fori_loop(0, devices, shrink, 0)
 
     def merge(b, carry):
         first = blocks[2 * b, :, pl.ds(2 * LANES, LANES)]
@@ -177,11 +191,11 @@
             for read in rows:
                 values = [jnp.broadcast_to(read(k), (8, LANES)) for k in range(6)]
                 for i in range(group):
-                    sums[i] = pair_terms(x[i], values[:3], values[3:], FAR_BLOB, sums[i])
+                    sums[i] = pair_terms(x[i], values[:3], values[3:], sums[i])
             return tuple(v for s in sums for v in s)
 
         flat = tuple(jnp.zeros((8, LANES), jnp.float32) for _ in range(3 * group))
-        flat = lax.fori_loop(0, devices // 2, sources, flat)
+        flat = lax.fori_loop(0, devices // 2, sources, flat, unroll=4)
         for i in range(group):
             for k in range(3):
                 sums_ref[k, pl.ds(starts[i], 8), :] = flat[3 * i + k]
@@ -194,7 +208,7 @@
             ones, sums_ref[k], (((1,), (1,)), ((), ())),
             precision=lax.Precision.HIGHEST, preferred_element_type=jnp.float32,
         )
-        velocity[k : k + 1, :] = total[:1] * np.float32(STOKES_FACTOR)
+        velocity[k : k + 1, :] = total[:1] * np.float32(STOKES_FACTOR / math.sqrt(FAR_BLOB))
 
 
 def greet(me, devices, inner):
@@ -215,8 +229,9 @@
     return {"blk": peer // inner, "tgt": lax.rem(peer, inner)}
 
 
-def interactions(entries, patches, devices, inner, target_ref, owner_ref, patch_ref, start_ref,
-                 listed_ref, zone_ref, own_ref, velocity, patch_velocity, blocks, coarse, fine, hot,
+def interactions(entries, patches, devices, inner, target_ref, owner_ref, patch_ref,
+                 named_ref, region_ref, rows_ref, zone_ref, position_ref, force_ref,
+                 velocity, patch_velocity, own_ref, start_vmem, start_ref, start_sem, blocks, coarse, fine, hot,
                  table, results, partial, landing, tails, sums_ref, sent, arrived, returned, landed):
     me = lax.axis_index("blk") * inner + lax.axis_index("tgt")
 
@@ -234,6 +249,9 @@
             device_id=address(me, step, devices, inner), device_id_type=MESH,
         )
 
+    own_ref[...] = jnp.zeros((8, WIDE), jnp.float32)
+    own_ref[0:3, 0:NODES] = position_ref[...]
+    own_ref[3:6, 0:NODES] = force_ref[...]
     greet(me, devices, inner)
 
     def start(step, carry):
@@ -242,8 +260,12 @@
 
     lax.fori_loop(1, devices, start, 0)
     blocks[me] = own_ref[...]
+    start_vmem[...] = jnp.broadcast_to(patch_starts(rows_ref[...]), (patches, LANES))
+    starts = pltpu.make_async_copy(start_vmem, start_ref, start_sem)
+    starts.start()
     upsample(own_ref[...].T, coarse, fine)
     zone_tables(patches, zone_ref, hot)
+    starts.wait()
 
     def arrive(step, carry):
         spread(step, lax.rem(me + devices - step, devices)).wait()
@@ -251,14 +273,14 @@
 
     lax.fori_loop(1, devices, arrive, 0)
     near_part(entries, patches, devices, target_ref, owner_ref, patch_ref, start_ref,
-              listed_ref, blocks, fine, hot, table, results, partial)
+              (named_ref, region_ref), blocks, fine, hot, table, results, partial)
 
     def start_back(step, carry):
         give_back(step, me).start()
         return carry
 
     lax.fori_loop(1, devices, start_back, 0)
-    far_part(devices, blocks, coarse, tails, sums_ref, velocity)
+    far_part(devices, own_ref, blocks, coarse, tails, sums_ref, velocity)
 
     def finish(step, total):
         slot = lax.rem(me + devices - step, devices)
@@ -269,13 +291,13 @@
     patch_velocity[...] = total[:3, :NODES]
 
 
-def patch_starts(patch_rows):
-    polar = jnp.min(patch_rows // FINE_PHI, axis=1)
-    around = patch_rows % FINE_PHI
-    lowest = jnp.min(around, axis=1)
-    wrapped = jnp.max(around, axis=1) - lowest >= SIDE
-    late = jnp.min(jnp.where(around >= FINE_PHI // 2, around, FINE_PHI), axis=1)
-    return polar * ROW + jnp.where(wrapped, late, lowest)
+def patch_starts(rows):
+    row = lax.shift_right_logical(rows * 14564, 20)
+    around = rows - row * FINE_PHI
+    lowest = jnp.min(around, axis=1, keepdims=True)
+    wrapped = jnp.max(around, axis=1, keepdims=True) - lowest >= SIDE
+    late = jnp.min(jnp.where(around >= FINE_PHI // 2, around, FINE_PHI), axis=1, keepdims=True)
+    return jnp.min(row, axis=1, keepdims=True) * ROW + jnp.where(wrapped, late, lowest)
 
 
 def on_device(
@@ -284,7 +306,6 @@
     devices = lax.axis_size(("blk", "tgt"))
     entries = near_target.shape[0]
     patches = patch_rows.shape[0]
-    own = jnp.pad(jnp.concatenate([positions, forces], axis=0), ((0, 2), (0, WIDE - NODES)))
     inner = lax.axis_size("tgt")
     smem = pl.BlockSpec(memory_space=pltpu.SMEM)
     vmem = pl.BlockSpec(memory_space=pltpu.VMEM)
@@ -292,9 +313,13 @@
     return pl.pallas_call(
         functools.partial(interactions, entries, patches, devices, inner),
         out_shape=(node_shape, node_shape),
-        in_specs=[smem] * 4 + [vmem] * 3,
+        in_specs=[smem] * 3 + [vmem] * 6,
         out_specs=(vmem, vmem),
         scratch_shapes=[
+            pltpu.VMEM((8, WIDE), jnp.float32),
+            pltpu.VMEM((patches, LANES), jnp.int32),
+            pltpu.SMEM((patches, LANES), jnp.int32),
+            pltpu.SemaphoreType.DMA,
             pltpu.VMEM((devices, 8, WIDE), jnp.float32),
             pltpu.VMEM((6, WIDE, LANES), jnp.float32),
             pltpu.VMEM((6, FINE_THETA * ROW, LANES), jnp.float32),
@@ -309,8 +334,8 @@
         compiler_params=pltpu.CompilerParams(
             collective_id=0, has_side_effects=True, vmem_limit_bytes=50 * 1024 * 1024
         ),
-    )(near_target, owner_map, near_patch, patch_starts(patch_rows),
-      jnp.stack([near_target, near_patch]), zone_rows, own)
+    )(near_target, owner_map, near_patch, near_target.reshape(1, entries),
+      near_patch.reshape(1, entries), patch_rows, zone_rows, positions, forces)
 
 
 def solution(mesh):

time: 52.3 us -> 50.7 us (0.969)
  Pallas kernels: 47.2 us -> 45 us
  local copies, waits for them, and re-layouts: 3.15 us -> 4.71 us
  other arithmetic: 0.98 us -> 0 us
    pallas_call x1, Pallas kernels: 47.2 us -> 45 us  [on_device(): pl.pallas_call(functools.partial(interactions, entries, patches, devices,...]
    unnamed x14 -> x16, local copies, waits for them, and re-layouts: 3.15 us -> 4.71 us
    reduce_min x1 -> x0, other arithmetic: 0.95 us -> none  [patch_starts(): polar = jnp.min(patch_rows // FINE_PHI, axis=1)]
where the time goes in v4:
time: 50.7 us; the launch traced here: 50.4 us
  Pallas kernels  45 us (89%)
  local copies, waits for them, and re-layouts  4.71 us (9%)
  between operations  0.67 us (1%)
    pallas_call x1, Pallas kernels, on_device(): pl.pallas_call(functools.partial(interactions, entries, patches, devices,...  45 us
    unnamed x16, local copies, waits for them, and re-layouts  4.71 us

profile of v4, /device:TPU:0, one launch (start us, length us, event | category | flops | bytes accessed | tf_op | source)
XLA Modules:
  0.0 50.4 jit_solution(2827904577047346609)
XLA Ops:
  0.6 0.0 copy-start.4
  0.6 0.0 copy-start.5
  0.7 0.0 copy-start.6
  0.7 0.6 %copy-done.4 = s32[128]{0:T(128)S(1)} copy-done((s32[128]{0:T(128)S(1)}, s32[128]{0:T(128)}, u32[]{:S(2)}) %copy-start.4) | copy-done | bytes 536
  1.3 0.0 copy-done.5
  1.3 0.0 copy-done.6
  1.3 0.0 copy-start
  1.3 0.8 %copy-done = s32[32,256]{1,0:T(8,128)S(1)} copy-done((s32[32,256]{1,0:T(8,128)S(1)}, s32[32,256]{1,0:T(8,128)}, u32[]{:S(2)}) %copy-start) | copy-done | bytes 32792
  2.1 0.0 copy-start.1
  2.1 0.7 %copy-done.1 = s32[32,128]{1,0:T(8,128)S(1)} copy-done((s32[32,128]{1,0:T(8,128)S(1)}, s32[32,128]{1,0:T(8,128)}, u32[]{:S(2)}) %copy-start.1) | copy-done | bytes 16408
  2.8 0.0 copy-start.2
  2.8 0.7 %copy-done.2 = f32[3,312]{1,0:T(4,128)S(1)} copy-done((f32[3,312]{1,0:T(4,128)S(1)}, f32[3,312]{1,0:T(4,128)}, u32[]{:S(2)}) %copy-start.2) | copy-done | bytes 3768
  3.5 0.0 copy-start.3
  3.5 0.7 %copy-done.3 = f32[3,312]{1,0:T(4,128)S(1)} copy-done((f32[3,312]{1,0:T(4,128)S(1)}, f32[3,312]{1,0:T(4,128)}, u32[]{:S(2)}) %copy-start.3) | copy-done | bytes 3768
  4.2 45.0 %shard_map.86 = (f32[3,312]{1,0:T(4,128)S(1)}, f32[3,312]{1,0:T(4,128)S(1)}) custom-call(s32[128]{0:T(128)S(1)} %copy-done.4, s32[16]{0:T(128)S(1)} %copy-done.6, s32[128]{0:T(128)S(1)} %copy-done.5, s32[1,128]{1,0:T(1,128)S(1)} %bitcast.2, s32[1,128]{1,0:T(1,128)S(1)} %bitcast.3, s32[32,256]{1,0:T(8,128)S(1)} %copy-done, s32[32,128]{1,0:T(8,128)S(1)} %copy-done.1, ...), custom_call_target="tpu_custom_call" | custom-call | tf_op jit(solution)/shard_map/pallas_call | solution.py:313
  49.2 0.6 %copy.11 = f32[3,312]{1,0:T(4,128)} copy(f32[3,312]{1,0:T(4,128)S(1)} %get-tuple-element.4) | data formatting | bytes 7488
  49.8 0.6 %copy.12 = f32[3,312]{1,0:T(4,128)} copy(f32[3,312]{1,0:T(4,128)S(1)} %get-tuple-element.5) | data formatting | bytes 7488
Async XLA Ops:
  0.6 0.7 %copy-start.4 = (s32[128]{0:T(128)S(1)}, s32[128]{0:T(128)}, u32[]{:S(2)}) copy-start(s32[128]{0:T(128)} %target_ref.1) | copy-start | bytes 1540
  0.6 0.7 %copy-start.5 = (s32[128]{0:T(128)S(1)}, s32[128]{0:T(128)}, u32[]{:S(2)}) copy-start(s32[128]{0:T(128)} %patch_ref.1) | copy-start | bytes 1540
  0.7 0.7 %copy-start.6 = (s32[16]{0:T(128)S(1)}, s32[16]{0:T(128)}, u32[]{:S(2)}) copy-start(s32[16]{0:T(128)} %owner_ref.1) | copy-start | bytes 196
  1.3 0.8 %copy-start = (s32[32,256]{1,0:T(8,128)S(1)}, s32[32,256]{1,0:T(8,128)}, u32[]{:S(2)}) copy-start(s32[32,256]{1,0:T(8,128)} %rows_ref.1) | copy-start | bytes 98308
  2.1 0.7 %copy-start.1 = (s32[32,128]{1,0:T(8,128)S(1)}, s32[32,128]{1,0:T(8,128)}, u32[]{:S(2)}) copy-start(s32[32,128]{1,0:T(8,128)} %zone_ref.1) | copy-start | bytes 49156
  2.8 0.7 %copy-start.2 = (f32[3,312]{1,0:T(4,128)S(1)}, f32[3,312]{1,0:T(4,128)}, u32[]{:S(2)}) copy-start(f32[3,312]{1,0:T(4,128)} %position_ref.1) | copy-start | bytes 11236
  3.5 0.7 %copy-start.3 = (f32[3,312]{1,0:T(4,128)S(1)}, f32[3,312]{1,0:T(4,128)}, u32[]{:S(2)}) copy-start(f32[3,312]{1,0:T(4,128)} %force_ref.1) | copy-start | bytes 11236

commit v5 on v4

--- a/solution.py
+++ b/solution.py
@@ -23,7 +23,7 @@
 FAR_BLOB = 0.09
 NEAR_BLOB = 0.0025
 STOKES_FACTOR = 1.0 / (8.0 * math.pi)
-ENTRIES_STEP = 4
+ENTRIES_STEP = 2
 MESH = pl.DeviceIdType.MESH
 
 
@@ -195,7 +195,7 @@
             return tuple(v for s in sums for v in s)
 
         flat = tuple(jnp.zeros((8, LANES), jnp.float32) for _ in range(3 * group))
-        flat = lax.fori_loop(0, devices // 2, sources, flat, unroll=4)
+        flat = lax.fori_loop(0, devices // 2, sources, flat, unroll=2)
         for i in range(group):
             for k in range(3):
                 sums_ref[k, pl.ds(starts[i], 8), :] = flat[3 * i + k]
@@ -230,8 +230,9 @@
 
 
 def interactions(entries, patches, devices, inner, target_ref, owner_ref, patch_ref,
-                 named_ref, region_ref, rows_ref, zone_ref, position_ref, force_ref,
-                 velocity, patch_velocity, own_ref, start_vmem, start_ref, start_sem, blocks, coarse, fine, hot,
+                 named_ref, region_ref, rows_hbm, zone_hbm, position_hbm, force_hbm,
+                 velocity, patch_velocity, rows_ref, zone_ref, position_ref, force_ref, load_sem,
+                 own_ref, start_vmem, start_ref, start_sem, blocks, coarse, fine, hot,
                  table, results, partial, landing, tails, sums_ref, sent, arrived, returned, landed):
     me = lax.axis_index("blk") * inner + lax.axis_index("tgt")
 
@@ -249,10 +250,17 @@
             device_id=address(me, step, devices, inner), device_id_type=MESH,
         )
 
+    pairs = ((position_hbm, position_ref), (force_hbm, force_ref),
+             (rows_hbm, rows_ref), (zone_hbm, zone_ref))
+    loads = [pltpu.make_async_copy(*pair, load_sem.at[i]) for i, pair in enumerate(pairs)]
+    for load in loads:
+        load.start()
+    greet(me, devices, inner)
     own_ref[...] = jnp.zeros((8, WIDE), jnp.float32)
+    loads[0].wait()
+    loads[1].wait()
     own_ref[0:3, 0:NODES] = position_ref[...]
     own_ref[3:6, 0:NODES] = force_ref[...]
-    greet(me, devices, inner)
 
     def start(step, carry):
         spread(step, me).start()
@@ -260,6 +268,8 @@
 
     lax.fori_loop(1, devices, start, 0)
     blocks[me] = own_ref[...]
+    loads[2].wait()
+    loads[3].wait()
     start_vmem[...] = jnp.broadcast_to(patch_starts(rows_ref[...]), (patches, LANES))
     starts = pltpu.make_async_copy(start_vmem, start_ref, start_sem)
     starts.start()
@@ -313,9 +323,14 @@
     return pl.pallas_call(
         functools.partial(interactions, entries, patches, devices, inner),
         out_shape=(node_shape, node_shape),
-        in_specs=[smem] * 3 + [vmem] * 6,
+        in_specs=[smem] * 3 + [vmem] * 2 + [pl.BlockSpec(memory_space=pl.ANY)] * 4,
         out_specs=(vmem, vmem),
         scratch_shapes=[
+            pltpu.VMEM(patch_rows.shape, jnp.int32),
+            pltpu.VMEM(zone_rows.shape, jnp.int32),
+            pltpu.VMEM(positions.shape, jnp.float32),
+            pltpu.VMEM(forces.shape, jnp.float32),
+            pltpu.SemaphoreType.DMA((4,)),
             pltpu.VMEM((8, WIDE), jnp.float32),
             pltpu.VMEM((patches, LANES), jnp.int32),
             pltpu.SMEM((patches, LANES), jnp.int32),

time: 50.7 us -> 51.4 us (1.014)
  Pallas kernels: 45 us -> 45.7 us
    pallas_call x1, Pallas kernels: 45 us -> 45.7 us  [on_device(): pl.pallas_call(functools.partial(interactions, entries, patches, devices,...]
where the time goes in v5:
time: 51.4 us; the launch traced here: 51.1 us
  Pallas kernels  45.7 us (89%)
  local copies, waits for them, and re-layouts  4.71 us (9%)
  between operations  0.67 us (1%)
    pallas_call x1, Pallas kernels, on_device(): pl.pallas_call(functools.partial(interactions, entries, patches, devices,...  45.7 us
    unnamed x16, local copies, waits for them, and re-layouts  4.71 us

profile of v5, /device:TPU:0, one launch (start us, length us, event | category | flops | bytes accessed | tf_op | source)
XLA Modules:
  0.0 51.1 jit_solution(14198358191695906598)
XLA Ops:
  0.6 0.0 copy-start.4
  0.6 0.0 copy-start.5
  0.7 0.0 copy-start.6
  0.7 0.6 %copy-done.4 = s32[128]{0:T(128)S(1)} copy-done((s32[128]{0:T(128)S(1)}, s32[128]{0:T(128)}, u32[]{:S(2)}) %copy-start.4) | copy-done | bytes 536
  1.3 0.0 copy-done.5
  1.3 0.0 copy-done.6
  1.3 0.0 copy-start
  1.3 0.8 %copy-done = s32[32,256]{1,0:T(8,128)S(1)} copy-done((s32[32,256]{1,0:T(8,128)S(1)}, s32[32,256]{1,0:T(8,128)}, u32[]{:S(2)}) %copy-start) | copy-done | bytes 32792
  2.1 0.0 copy-start.1
  2.1 0.7 %copy-done.1 = s32[32,128]{1,0:T(8,128)S(1)} copy-done((s32[32,128]{1,0:T(8,128)S(1)}, s32[32,128]{1,0:T(8,128)}, u32[]{:S(2)}) %copy-start.1) | copy-done | bytes 16408
  2.8 0.0 copy-start.2
  2.8 0.7 %copy-done.2 = f32[3,312]{1,0:T(4,128)S(1)} copy-done((f32[3,312]{1,0:T(4,128)S(1)}, f32[3,312]{1,0:T(4,128)}, u32[]{:S(2)}) %copy-start.2) | copy-done | bytes 3768
  3.5 0.0 copy-start.3
  3.5 0.7 %copy-done.3 = f32[3,312]{1,0:T(4,128)S(1)} copy-done((f32[3,312]{1,0:T(4,128)S(1)}, f32[3,312]{1,0:T(4,128)}, u32[]{:S(2)}) %copy-start.3) | copy-done | bytes 3768
  4.2 45.7 %shard_map.86 = (f32[3,312]{1,0:T(4,128)S(1)}, f32[3,312]{1,0:T(4,128)S(1)}) custom-call(s32[128]{0:T(128)S(1)} %copy-done.4, s32[16]{0:T(128)S(1)} %copy-done.6, s32[128]{0:T(128)S(1)} %copy-done.5, s32[1,128]{1,0:T(1,128)S(1)} %bitcast.2, s32[1,128]{1,0:T(1,128)S(1)} %bitcast.3, s32[32,256]{1,0:T(8,128)S(1)} %copy-done, s32[32,128]{1,0:T(8,128)S(1)} %copy-done.1, ...), custom_call_target="tpu_custom_call" | custom-call | tf_op jit(solution)/shard_map/pallas_call | solution.py:323
  49.9 0.6 %copy.11 = f32[3,312]{1,0:T(4,128)} copy(f32[3,312]{1,0:T(4,128)S(1)} %get-tuple-element.4) | data formatting | bytes 7488
  50.5 0.6 %copy.12 = f32[3,312]{1,0:T(4,128)} copy(f32[3,312]{1,0:T(4,128)S(1)} %get-tuple-element.5) | data formatting | bytes 7488
Async XLA Ops:
  0.6 0.7 %copy-start.4 = (s32[128]{0:T(128)S(1)}, s32[128]{0:T(128)}, u32[]{:S(2)}) copy-start(s32[128]{0:T(128)} %target_ref.1) | copy-start | bytes 1540
  0.6 0.7 %copy-start.5 = (s32[128]{0:T(128)S(1)}, s32[128]{0:T(128)}, u32[]{:S(2)}) copy-start(s32[128]{0:T(128)} %patch_ref.1) | copy-start | bytes 1540
  0.7 0.7 %copy-start.6 = (s32[16]{0:T(128)S(1)}, s32[16]{0:T(128)}, u32[]{:S(2)}) copy-start(s32[16]{0:T(128)} %owner_ref.1) | copy-start | bytes 196
  1.3 0.8 %copy-start = (s32[32,256]{1,0:T(8,128)S(1)}, s32[32,256]{1,0:T(8,128)}, u32[]{:S(2)}) copy-start(s32[32,256]{1,0:T(8,128)} %rows_hbm.1) | copy-start | bytes 98308
  2.1 0.7 %copy-start.1 = (s32[32,128]{1,0:T(8,128)S(1)}, s32[32,128]{1,0:T(8,128)}, u32[]{:S(2)}) copy-start(s32[32,128]{1,0:T(8,128)} %zone_hbm.1) | copy-start | bytes 49156
  2.8 0.7 %copy-start.2 = (f32[3,312]{1,0:T(4,128)S(1)}, f32[3,312]{1,0:T(4,128)}, u32[]{:S(2)}) copy-start(f32[3,312]{1,0:T(4,128)} %position_hbm.1) | copy-start | bytes 11236
  3.5 0.7 %copy-start.3 = (f32[3,312]{1,0:T(4,128)S(1)}, f32[3,312]{1,0:T(4,128)}, u32[]{:S(2)}) copy-start(f32[3,312]{1,0:T(4,128)} %force_hbm.1) | copy-start | bytes 11236
